TPU v7x, 32 devices: a whole 2x2x4 slice. The times are simulated.
32 devices in a mesh: table: 8 (over y, x, core), sample: 4 (over z).
Axes of the slice: x: 2, y: 2, z: 4, core: 2. Of those that a mesh axis runs over, the one named last changes fastest.
Arguments:
- hist_ids: int32 [512, 8, 48], P(('table', 'sample')), may hold values from 0 to 2047
- hist_lens: int32 [512, 8], P(('table', 'sample')), may hold values from 1 to 48, 256 in all within a row
- table_rows: bfloat16 [16384, 256], P('table'), may hold values from -6 to 6
- imp_user: int32 [8192], P(('table', 'sample')), may hold values from 0 to 63
- item_rows: bfloat16 [8192, 256], P(('table', 'sample')), may hold values from -6 to 6
- labels: int32 [8192], P(('table', 'sample')), may hold values 0 or 1
- w_hidden: bfloat16 [512, 512], replicated, may hold values from -0.25 to 0.25
- b_hidden: float32 [512], replicated, may hold values from -3 to 3
- w_back: bfloat16 [512, 512], replicated, may hold values from -0.25 to 0.25
- w_cross: bfloat16 [512, 512], replicated, may hold values from -0.25 to 0.25
- b_cross: float32 [512], replicated, may hold values from -4 to 4
- norm_gain: float32 [512], replicated, may hold values from 0.25 to 1.75
- w_score: float32 [512], replicated, may hold values from -0.25 to 0.25
Outputs:
- pooled_user: bfloat16 [512, 256], P(('table', 'sample'))
- scores: float32 [8192], P(('table', 'sample'))
- user_grad: float32 [512, 256], P(('table', 'sample'))
- item_grad: float32 [8192, 256], P(('table', 'sample'))
Inputs may be any that keep to these rules, and one draw needn't show every extreme that they name: `hist_lens`: each user's live ids over all shards number exactly 256; some user has 48 live ids in one shard. `imp_user`: an impression names one of the 64 users held by the devices of its own table index.
All inputs are finite; a program needn't handle non-finite values. No bound on the sum of `labels` on one device may be relied on, other than what follows from the above.
Results may differ from a plain program's by a relative error of at most 0.02.
Values may be sent and summed in bfloat16 or wider, within the bound.
A program may use at most 64 MiB of HBM per device.

v0:
```python
import math

import jax
import jax.numpy as jnp
from jax import lax
from jax.sharding import PartitionSpec as P


def forward(user_in, item_in, w_hidden, b_hidden, w_back, w_cross, b_cross, norm_gain, w_score):
    joined = jnp.concatenate([user_in, item_in], axis=1).astype(jnp.bfloat16)
    hidden = jax.nn.gelu(
        jnp.dot(joined, w_hidden, preferred_element_type=jnp.float32) + b_hidden
    ).astype(jnp.bfloat16)
    mlp_out = jnp.dot(hidden, w_back, preferred_element_type=jnp.float32)
    lifted = joined.astype(jnp.float32)
    crossed = lifted * (jnp.dot(joined, w_cross, preferred_element_type=jnp.float32) + b_cross)
    summed = lifted + mlp_out + crossed
    row_mean = jnp.mean(summed, axis=1, keepdims=True)
    centred = summed - row_mean
    row_var = jnp.mean(centred * centred, axis=1, keepdims=True)
    normed = centred * lax.rsqrt(row_var + 1e-05) * norm_gain
    return jnp.dot(normed, w_score, precision=lax.Precision.HIGHEST)


def body(
    hist_ids,
    hist_lens,
    table_rows,
    imp_user,
    item_rows,
    labels,
    w_hidden,
    b_hidden,
    w_back,
    w_cross,
    b_cross,
    norm_gain,
    w_score,
):
    width = table_rows.shape[1]
    table_count = table_rows.shape[0]
    slot_count = hist_ids.shape[2]
    users_here = hist_ids.shape[0]
    sources = lax.axis_size("table")
    history = slot_count * sources * 2 // 3
    recv_ids = lax.all_to_all(hist_ids, "table", split_axis=1, concat_axis=1, tiled=True)
    recv_lens = lax.all_to_all(hist_lens, "table", split_axis=1, concat_axis=1, tiled=True)
    items = recv_ids.shape[0]
    group = math.gcd(sources, max(1, 128 // max(1, items)))
    blocks_count = sources // group
    flat_ids = jnp.transpose(recv_ids, (1, 0, 2)).reshape(blocks_count, group * items, slot_count)
    flat_lens = jnp.transpose(recv_lens, (1, 0)).reshape(blocks_count, group * items)

    def pool_block(pair):
        block_ids, block_lens = pair
        live_slots = lax.broadcasted_iota(jnp.int32, block_ids.shape, 1) < block_lens[:, None]
        masked_ids = jnp.where(live_slots, block_ids, -1)
        row_iota = lax.broadcasted_iota(jnp.int32, (1, 1, table_count), 2)
        counts = jnp.sum((masked_ids[:, :, None] == row_iota).astype(jnp.float32), axis=1).astype(
            jnp.bfloat16
        )
        return jnp.dot(counts, table_rows, preferred_element_type=jnp.float32)

    pooled_blocks = lax.map(pool_block, (flat_ids, flat_lens))
    partials = jnp.transpose(pooled_blocks.reshape(sources, items, width), (1, 0, 2))
    returned = lax.all_to_all(partials, "table", split_axis=1, concat_axis=1, tiled=True)
    pooled_user = (jnp.sum(returned, axis=1) * float(history) ** (-0.5)).astype(jnp.bfloat16)
    shard_part = lax.all_gather(pooled_user, "sample", axis=0, tiled=True)
    picks = (
        imp_user[:, None] == lax.broadcasted_iota(jnp.int32, (1, shard_part.shape[0]), 1)
    ).astype(jnp.bfloat16)
    expanded = jnp.dot(picks, shard_part, preferred_element_type=jnp.float32)
    user_feat = expanded.astype(jnp.bfloat16)

    def score_of(user_in, item_in):
        return forward(
            user_in, item_in, w_hidden, b_hidden, w_back, w_cross, b_cross, norm_gain, w_score
        )

    scores, pullback = jax.vjp(
        score_of, user_feat.astype(jnp.float32), item_rows.astype(jnp.float32)
    )
    score_grad = jax.nn.sigmoid(scores) - labels.astype(jnp.float32)
    user_part, item_grad = pullback(score_grad)
    group_users = users_here * lax.axis_size("sample")
    picks = (imp_user[:, None] == lax.broadcasted_iota(jnp.int32, (1, group_users), 1)).astype(
        jnp.float32
    )
    per_user = jnp.einsum("ru,re->ue", picks, user_part, precision=lax.Precision.HIGHEST)
    user_grad = lax.psum_scatter(
        per_user.astype(jnp.bfloat16), "sample", scatter_dimension=0, tiled=True
    ).astype(jnp.float32)
    return (pooled_user, scores, user_grad, item_grad)


def solution(mesh):
    in_specs = (
        P(("table", "sample"), None, None),
        P(("table", "sample"), None),
        P("table", None),
        P(("table", "sample")),
        P(("table", "sample"), None),
        P(("table", "sample")),
        P(),
        P(),
        P(),
        P(),
        P(),
        P(),
        P(),
    )
    out_specs = (
        P(("table", "sample"), None),
        P(("table", "sample")),
        P(("table", "sample"), None),
        P(("table", "sample"), None),
    )
    return jax.shard_map(body, mesh=mesh, in_specs=in_specs, out_specs=out_specs, check_vma=False)
```

profile of v0, /device:TPU:0, one launch (start us, length us, event | category | flops | bytes accessed | tf_op | source)
XLA Modules:
  0.0 96.0 jit_solution(13513487487205393642)
XLA Ops:
  7.2 0.0 copy-start
  7.2 5.3 %all-to-all-start = ((s32[16,8,1]{0,2,1:T(1,128)}), s32[16,8,1]{0,2,1:T(1,128)S(1)}, u32[]{:S(2)}, u32[]{:S(2)}) async-start(s32[16,8,1]{0,2,1:T(1,128)} %bitcast.35), calls=%async_computation | async-start | bytes 8192 | tf_op jit(solution)/shard_map/all_to_all | solution.py:47
  12.5 0.9 copy.51
  13.4 0.7 reshape.77
  14.1 3.0 %all-to-all-done = s32[16,8,1]{0,2,1:T(1,128)S(1)} async-done(((s32[16,8,1]{0,2,1:T(1,128)}), s32[16,8,1]{0,2,1:T(1,128)S(1)}, u32[]{:S(2)}, u32[]{:S(2)}) %all-to-all-start) | async-done | bytes 544 | tf_op jit(solution)/shard_map/all_to_all | solution.py:47
  17.1 3.3 %all-to-all-start.1 = ((s32[8,1,768]{2,1,0:T(1,128)}), s32[8,1,768]{2,1,0:T(1,128)S(1)}, u32[]{:S(2)}, u32[]{:S(2)}) async-start(s32[8,1,768]{2,1,0:T(1,128)} %reshape.77), calls=%async_computation.1 | async-start | bytes 49152 | tf_op jit(solution)/shard_map/all_to_all | solution.py:46
  20.4 0.1 lt.19
  20.5 4.7 %all-to-all-done.1 = s32[8,1,768]{2,1,0:T(1,128)S(1)} async-done(((s32[8,1,768]{2,1,0:T(1,128)}), s32[8,1,768]{2,1,0:T(1,128)S(1)}, u32[]{:S(2)}, u32[]{:S(2)}) %all-to-all-start.1) | async-done | bytes 24608 | tf_op jit(solution)/shard_map/all_to_all | solution.py:46
  25.2 0.5 broadcast.125
  25.7 0.7 reduce
  26.4 0.1 reshape.78
  26.5 0.1 bitcast_select_fusion
  26.6 12.3 %convert_reduce_fusion = bf16[128,2048]{1,0:T(8,128)(2,1)S(1)} fusion(s32[128,48]{1,0:T(8,128)S(1)} %bitcast_select_fusion), kind=kLoop, calls=%fused_computation | loop fusion | flops 37486592 | bytes 548864 | tf_op jit(solution)/shard_map/while/body/eval_jaxpr/reduce_sum | solution.py:59
  38.9 0.0 copy-done
  38.9 0.0 copy-start.3
  38.9 0.0 copy-start.10
  38.9 0.0 copy-start.2
  39.0 0.0 copy-start.8
  39.0 1.0 %fusion.67 = f32[128,256]{1,0:T(8,128)} fusion(bf16[128,2048]{1,0:T(8,128)(2,1)S(1)} %convert_reduce_fusion, bf16[2048,256]{1,0:T(8,128)(2,1)S(1)} %copy-done), kind=kOutput, calls=%fused_computation.94 | convolution fusion | flops 134217728 | bytes 1703936 | tf_op jit(solution)/shard_map/while/body/eval_jaxpr/dot_general | solution.py:62
  39.9 3.5 %all-to-all-start.2 = ((f32[16,8,256]{2,0,1:T(8,128)}), f32[16,8,256]{2,0,1:T(8,128)S(1)}, u32[]{:S(2)}, u32[]{:S(2)}) async-start(f32[16,8,256]{2,0,1:T(8,128)} %bitcast.7), calls=%async_computation.2 | async-start | bytes 262144 | tf_op jit(solution)/shard_map/all_to_all | solution.py:66
  43.5 0.0 reduce-scatter.2.cloned.1.call-start
  43.5 0.1 copy.40
  43.6 5.3 %all-to-all-done.2 = f32[16,8,256]{2,0,1:T(8,128)S(1)} async-done(((f32[16,8,256]{2,0,1:T(8,128)}), f32[16,8,256]{2,0,1:T(8,128)S(1)}, u32[]{:S(2)}, u32[]{:S(2)}) %all-to-all-start.2) | async-done | bytes 131104 | tf_op jit(solution)/shard_map/all_to_all | solution.py:66
  48.9 0.0 copy-start.4
  49.0 13.4 %all_gather.3 = bf16[64,256]{1,0:T(8,128)(2,1)S(1)} all-gather(bf16[16,256]{1,0:T(8,128)(2,1)S(1)} %multiply_convert_fusion.2), channel_id=1, replica_groups=mesh['table'=8,'sample'=4] {'sample'}, dimensions={0}, use_global_device_ids=true | all-gather | bytes 40960 | tf_op jit(solution)/shard_map/all_gather | solution.py:68
  62.3 0.0 copy-done.10
  62.3 0.3 convolution_convert_fusion.3
  62.6 0.0 copy-start.12
  62.6 0.3 convolution_add_fusion.2
  63.0 0.4 convolution_add_fusion
  63.4 0.0 copy-done.4
  63.4 0.3 copy-done.12
  63.7 0.5 fusion.66
  64.2 0.0 copy-start.11
  64.2 0.1 multiply_reduce_fusion.1
  64.3 0.0 copy-done.5
  64.3 0.0 copy-done.6
  64.4 0.4 fusion.21
  64.8 0.1 copy-done.11
  64.8 0.2 multiply_reduce_fusion
  65.1 0.2 fusion.65
  65.3 1.3 %fusion.2 = bf16[256,512]{0,1:T(8,128)(2,1)} fusion(bf16[512,512]{1,0:T(8,128)(2,1)S(1)} %copy-done.1, f32[256,512]{0,1:T(8,128)S(1)} %convolution_add_fusion, f32[256]{0:T(256)S(1)} %negate_multiply_fusion, bf16[256,256]{0,1:T(8,128)(2,1)S(1)} %copy.40, bf16[256,256]{0,1:T(8,128)(2,1)S(1)} %convolution_convert_fusion.3, ...), kind=kOutput, calls=%fused_computation.10 | convolution fusion | flops 137625600 | bytes 2106368 | tf_op jit(solution)/shard_map/transpose(jvp())/dot_general | solution.py:16
  66.6 2.2 %fusion.3 = bf16[256,512]{0,1:T(8,128)(2,1)S(1)} fusion(bf16[256,512]{0,1:T(8,128)(2,1)} %fusion.2, bf16[512,512]{1,0:T(8,128)(2,1)S(1)} %copy-done.2, f32[256,512]{1,0:T(8,128)S(1)} %convolution_add_fusion.2, bf16[512,512]{1,0:T(8,128)(2,1)} %param.21, f32[256]{0:T(256)S(1)} %negate_multiply_fusion, f32[256,512]{0,1:T(8,128)S(1)} %get-tuple-element.36, ...), kind=kOutput, calls=%fused_computation.11 | convolution fusion | flops 272891904 | bytes 2630656 | tf_op jit(solution)/shard_map/transpose(jvp())/dot_general | solution.py:12
  68.7 0.9 convolution_convert_fusion.4
  69.6 0.0 reduce-scatter.2.cloned.1.call-update
  69.7 0.8 copy.45
  70.5 17.4 %reduce-scatter.2.cloned.1.call-done = bf16[16,256]{1,0:T(8,128)(2,1)} async-done(((bf16[64,256]{1,0:T(8,128)(2,1)}), bf16[16,256]{1,0:T(8,128)(2,1)}) %reduce-scatter.2.cloned.1.call-update) | async-done | bytes 8208 | tf_op jit(solution)/shard_map/reduce_scatter | solution.py:90
  87.9 1.3 %convert_element_type.63 = f32[16,256]{1,0:T(8,128)} convert(bf16[16,256]{1,0:T(8,128)(2,1)} %reduce-scatter.2.cloned.1.call-done) | non-fusion elementwise | flops 4096 | bytes 24576 | tf_op jit(solution)/shard_map/convert_element_type | solution.py:92
  (19 shorter events, 0.1 us)
Async XLA Ops:
  7.2 31.7 %copy-start = (bf16[2048,256]{1,0:T(8,128)(2,1)S(1)}, bf16[2048,256]{1,0:T(8,128)(2,1)}, u32[]{:S(2)}) copy-start(bf16[2048,256]{1,0:T(8,128)(2,1)} %param.15) | copy-start | bytes 3145732
  7.2 9.9 %all-to-all-start = ((s32[16,8,1]{0,2,1:T(1,128)}), s32[16,8,1]{0,2,1:T(1,128)S(1)}, u32[]{:S(2)}, u32[]{:S(2)}) async-start(s32[16,8,1]{0,2,1:T(1,128)} %bitcast.35), calls=%async_computation | async-start | bytes 8192 | tf_op jit(solution)/shard_map/all_to_all | solution.py:47
  17.1 8.1 %all-to-all-start.1 = ((s32[8,1,768]{2,1,0:T(1,128)}), s32[8,1,768]{2,1,0:T(1,128)S(1)}, u32[]{:S(2)}, u32[]{:S(2)}) async-start(s32[8,1,768]{2,1,0:T(1,128)} %reshape.77), calls=%async_computation.1 | async-start | bytes 49152 | tf_op jit(solution)/shard_map/all_to_all | solution.py:46
  38.9 4.6 %copy-start.3 = (bf16[256,256]{1,0:T(8,128)(2,1)S(1)}, bf16[256,256]{1,0:T(8,128)(2,1)}, u32[]{:S(2)}) copy-start(bf16[256,256]{1,0:T(8,128)(2,1)} %param.17) | copy-start | bytes 393220
  38.9 23.4 %copy-start.10 = (s32[256]{0:T(256)S(1)}, s32[256]{0:T(256)}, u32[]{:S(2)}) copy-start(s32[256]{0:T(256)} %param.16) | copy-start | bytes 3076
  38.9 23.7 %copy-start.2 = (bf16[512,512]{1,0:T(8,128)(2,1)S(1)}, bf16[512,512]{1,0:T(8,128)(2,1)}, u32[]{:S(2)}) copy-start(bf16[512,512]{1,0:T(8,128)(2,1)} %param.19) | copy-start | bytes 1572868
  39.0 23.7 %copy-start.8 = (f32[512]{0:T(512)S(1)}, f32[512]{0:T(512)}, u32[]{:S(2)}) copy-start(f32[512]{0:T(512)} %param.20) | copy-start | bytes 6148
  39.9 23.0 %copy-start.1 = (bf16[512,512]{1,0:T(8,128)(2,1)S(1)}, bf16[512,512]{1,0:T(8,128)(2,1)}, u32[]{:S(2)}) copy-start(bf16[512,512]{1,0:T(8,128)(2,1)} %param.22) | copy-start | bytes 1572868
  39.9 23.0 %copy-start.9 = (f32[512]{0:T(512)S(1)}, f32[512]{0:T(512)}, u32[]{:S(2)}) copy-start(f32[512]{0:T(512)} %param.23) | copy-start | bytes 6148
  39.9 9.0 %all-to-all-start.2 = ((f32[16,8,256]{2,0,1:T(8,128)}), f32[16,8,256]{2,0,1:T(8,128)S(1)}, u32[]{:S(2)}, u32[]{:S(2)}) async-start(f32[16,8,256]{2,0,1:T(8,128)} %bitcast.7), calls=%async_computation.2 | async-start | bytes 262144 | tf_op jit(solution)/shard_map/all_to_all | solution.py:66
  43.5 44.4 %reduce-scatter.2.cloned.1.call-start = ((), (), s32[]{:S(2)}) async-start(), calls=%async_computation.4 | async-start | bytes 40960 | tf_op jit(solution)/shard_map/reduce_scatter | solution.py:90
  48.9 14.4 %copy-start.4 = (bf16[16,256]{1,0:T(8,128)(2,1)}, bf16[16,256]{1,0:T(8,128)(2,1)S(1)}, u32[]{:S(2)}) copy-start(bf16[16,256]{1,0:T(8,128)(2,1)S(1)} %multiply_convert_fusion.2) | copy-start | bytes 24580
  62.6 1.0 %copy-start.12 = (bf16[512,512]{1,0:T(8,128)(2,1)S(1)}, bf16[512,512]{1,0:T(8,128)(2,1)}, u32[]{:S(2)}) copy-start(bf16[512,512]{1,0:T(8,128)(2,1)} %param.21) | copy-start | bytes 1572868
  63.7 0.7 copy-start.5
  63.7 0.7 copy-start.6
  64.2 0.7 copy-start.11
  64.8 1.8 %copy-start.7 = (f32[1,256]{1,0:T(1,128)}, f32[1,256]{1,0:T(1,128)S(1)}, u32[]{:S(2)}) copy-start(f32[1,256]{1,0:T(1,128)S(1)} %fusion.21) | copy-start | bytes 3076
Sparse Core Ops, SparseCore 0:
  69.8 18.0 reduce-scatter.1
where the time goes:
time: 96.6 us; the launch traced here: 96 us
  waiting for transfers between devices  30.3 us (31%)
  other arithmetic  15.1 us (16%)
  between operations  14.3 us (15%)
  blocking collectives  13.4 us (14%)
  starting transfers between devices  12.2 us (13%)
  matrix products  7.13 us (7%)
  local copies, waits for them, and re-layouts  3.66 us (4%)
    reduce_scatter x1, waiting for transfers between devices, body(): lax.psum_scatter(per_user.astype(jnp.bfloat16), 'sample', scatter_dimensi...  17.4 us
    all_gather x1, blocking collectives, body(): shard_part = lax.all_gather(pooled_user, 'sample', axis=0, tiled=True)  13.4 us
    reduce_sum x1, other arithmetic, pool_block(): jnp.sum((masked_ids[:, :, None] == row_iota).astype(jnp.float32), axis=1)  12.3 us
    all_to_all x1, starting transfers between devices, body(): lax.all_to_all(hist_lens, 'table', split_axis=1, concat_axis=1, tiled=True)  5.31 us
    all_to_all x1, waiting for transfers between devices, body(): lax.all_to_all(partials, 'table', split_axis=1, concat_axis=1, tiled=True)  5.3 us
    all_to_all x1, waiting for transfers between devices, body(): lax.all_to_all(hist_ids, 'table', split_axis=1, concat_axis=1, tiled=True)  4.65 us
    all_to_all x1, starting transfers between devices, body(): lax.all_to_all(partials, 'table', split_axis=1, concat_axis=1, tiled=True)  3.5 us
    all_to_all x1, starting transfers between devices, body(): lax.all_to_all(hist_ids, 'table', split_axis=1, concat_axis=1, tiled=True)  3.34 us
  transfers between devices with their start and end apart: 4, of which 4 were waited for; matrix products, arithmetic and copies ran while one was open for 3% of the time, Pallas kernels for 0%

commit v1 on v0

v1 whole, which is shorter than its diff:
```python
import functools

import jax
import jax.numpy as jnp
from jax import lax
from jax.experimental import pallas as pl
from jax.experimental.pallas import tpu as pltpu
from jax.sharding import PartitionSpec as P

MESH = pl.DeviceIdType.MESH
F32 = jnp.float32
BF16 = jnp.bfloat16
LANES = 128
GELU_A = 0.7978845608028654
GELU_B = 0.044715


def dot_nn(a, b):
    return lax.dot_general(a, b, (((1,), (0,)), ((), ())), preferred_element_type=F32)


def dot_nt(a, b):
    return lax.dot_general(a, b, (((1,), (1,)), ((), ())), preferred_element_type=F32)


def to_column(row, width):
    return jnp.transpose(jnp.broadcast_to(row, (width, row.shape[1])))


def each(count, body):
    if count <= 8:
        for i in range(count):
            body(i)
    else:
        lax.fori_loop(0, count, lambda i, c: (body(i), c)[1], 0)


def kernel(
    scale,
    ids_ref,
    lens_ref,
    table_hbm,
    imp_ref,
    item_hbm,
    label_ref,
    wh_hbm,
    bh_ref,
    wb_hbm,
    wc_hbm,
    bc_ref,
    gain_ref,
    ws_ref,
    pooled_out,
    scores_out,
    ugrad_out,
    igrad_hbm,
    table_v,
    item_v,
    wh_v,
    wb_v,
    wc_v,
    msg,
    got,
    counts,
    part_send,
    part_recv,
    pool_all,
    grad_send,
    grad_recv,
    igrad_v,
    load_sem,
    ids_ssem,
    ids_rsem,
    part_ssem,
    part_rsem,
    pool_ssem,
    pool_rsem,
    grad_ssem,
    grad_rsem,
):
    tables, chunks = msg.shape[0], msg.shape[1]
    samples = pool_all.shape[0]
    users, _, slots = ids_ref.shape
    width = table_v.shape[1]
    n_hi = table_v.shape[0] // LANES
    imps = item_v.shape[0]
    group = samples * users
    t = lax.axis_index("table")
    s = lax.axis_index("sample")

    def table_peer(d):
        return lax.rem(t + d, tables)

    def sample_peer(d):
        return lax.rem(s + d, samples)

    barrier = pltpu.get_barrier_semaphore()

    def greet_table(i):
        pl.semaphore_signal(barrier, inc=1, device_id=(table_peer(i + 1), s), device_id_type=MESH)

    def greet_sample(i):
        pl.semaphore_signal(barrier, inc=1, device_id=(t, sample_peer(i + 1)), device_id_type=MESH)

    each(tables - 1, greet_table)
    each(samples - 1, greet_sample)

    loads = [
        pltpu.make_async_copy(src, dst, load_sem.at[i])
        for i, (src, dst) in enumerate(
            [
                (table_hbm, table_v),
                (item_hbm, item_v),
                (wh_hbm, wh_v),
                (wc_hbm, wc_v),
                (wb_hbm, wb_v),
            ]
        )
    ]
    for load in loads:
        load.start()

    eye = lax.broadcasted_iota(jnp.int32, (tables, tables), 0) == lax.broadcasted_iota(
        jnp.int32, (tables, tables), 1
    )
    slot_iota = lax.broadcasted_iota(jnp.int32, (tables, slots), 1)
    pieces = []
    for u in range(users):
        lens_u = jnp.broadcast_to(lens_ref[u : u + 1, :], (tables, tables))
        len_col = jnp.sum(jnp.where(eye, lens_u, 0), axis=1, keepdims=True)
        pieces.append(jnp.where(slot_iota < len_col, ids_ref[u], -1))
    packed = jnp.concatenate(pieces, axis=1)
    for c in range(users * slots // LANES):
        msg[:, c, :] = packed[:, c * LANES : (c + 1) * LANES]
    for c in range(users * slots // LANES, chunks):
        msg[:, c, :] = jnp.full((tables, LANES), -1, jnp.int32)

    pl.semaphore_wait(barrier, tables - 1 + samples - 1)

    def ids_copy(dst_table, owner, src_table):
        return pltpu.make_async_remote_copy(
            src_ref=msg.at[src_table],
            dst_ref=got.at[owner],
            send_sem=ids_ssem.at[src_table],
            recv_sem=ids_rsem.at[owner],
            device_id=(dst_table, s),
            device_id_type=MESH,
        )

    def send_ids(i):
        peer = table_peer(i + 1)
        ids_copy(peer, t, peer).start()

    each(tables - 1, send_ids)
    got[t] = msg[t]

    imp_row = imp_ref[...].astype(F32)
    imp_col = to_column(imp_row, LANES)[:, :1]
    picks = jnp.where(
        imp_col == lax.broadcasted_iota(jnp.int32, (imps, group), 1).astype(F32), 1.0, 0.0
    ).astype(BF16)
    picks_t = jnp.where(
        imp_ref[...] == lax.broadcasted_iota(jnp.int32, (group, imps), 0), 1.0, 0.0
    ).astype(BF16)
    label_col = to_column(label_ref[...].astype(F32), LANES)[:, :1]
    v_row = gain_ref[...] * ws_ref[...]
    v_centred = v_row - jnp.mean(v_row, axis=1, keepdims=True)

    position = (
        lax.broadcasted_iota(jnp.int32, (chunks, LANES), 0) * LANES
        + lax.broadcasted_iota(jnp.int32, (chunks, LANES), 1)
    )
    user_of = jnp.zeros((chunks, LANES), jnp.int32)
    for u in range(1, users):
        user_of = user_of + jnp.where(position >= u * slots, 1, 0)
    hi_iota = lax.broadcasted_iota(jnp.int32, (n_hi * users, LANES), 0)
    lo_iota = lax.broadcasted_iota(jnp.int32, (LANES, LANES), 0)
    used = users * slots // LANES

    def count_source(i):
        source = lax.rem(t + tables - i, tables)
        if isinstance(i, int):
            if i > 0:
                ids_copy(t, source, t).wait_recv()
        else:

            @pl.when(i > 0)
            def _():
                ids_copy(t, source, t).wait_recv()

        ids = got[source]
        hi_key = jnp.where(ids >= 0, (ids >> 7) * users + user_of, -1)
        lo_key = ids & (LANES - 1)
        hi_hot, lo_hot = [], []
        for c in range(used):
            hi_hot.append(jnp.where(hi_key[c : c + 1, :] == hi_iota, 1.0, 0.0).astype(BF16))
            lo_hot.append(jnp.where(lo_key[c : c + 1, :] == lo_iota, 1.0, 0.0).astype(BF16))
        block = dot_nt(jnp.concatenate(hi_hot, axis=1), jnp.concatenate(lo_hot, axis=1))
        block = block.astype(BF16)
        rows = pl.ds(pl.multiple_of(source * users, users), users)
        for h in range(n_hi):
            counts[rows, h * LANES : (h + 1) * LANES] = block[h * users : (h + 1) * users, :]

    each(tables, count_source)

    loads[0].wait()
    per_step = min(tables, 8)
    table_all = table_v[...]

    def pool_step(k):
        rows = per_step * users
        part = dot_nn(counts[pl.ds(k * rows, rows), :], table_all).astype(BF16)
        part_send[pl.ds(k * per_step, per_step)] = part.reshape(per_step, users, width)

    each(tables // per_step, pool_step)

    def part_copy(dst_table, owner, src_table):
        return pltpu.make_async_remote_copy(
            src_ref=part_send.at[src_table],
            dst_ref=part_recv.at[owner],
            send_sem=part_ssem.at[src_table],
            recv_sem=part_rsem.at[owner],
            device_id=(dst_table, s),
            device_id_type=MESH,
        )

    def send_part(i):
        peer = table_peer(i + 1)
        part_copy(peer, t, peer).start()

    each(tables - 1, send_part)
    part_recv[t] = part_send[t]

    loads[1].wait()
    loads[2].wait()
    loads[3].wait()
    items = item_v[...]
    half = width
    pre_item = dot_nn(items, wh_v[half:, :]) + bh_ref[...]
    cross_item = dot_nn(items, wc_v[half:, :]) + (bc_ref[...] + 1.0)

    def take_part(i):
        source = lax.rem(t + tables - 1 - i, tables)
        part_copy(t, source, t).wait_recv()

    each(tables - 1, take_part)
    pooled = jnp.sum(part_recv[...].astype(F32), axis=0) * scale
    pooled = pooled.astype(BF16)
    pool_all[s] = pooled

    def pool_copy(dst_sample, owner, sem):
        return pltpu.make_async_remote_copy(
            src_ref=pool_all.at[owner],
            dst_ref=pool_all.at[owner],
            send_sem=pool_ssem.at[sem],
            recv_sem=pool_rsem.at[owner],
            device_id=(t, dst_sample),
            device_id_type=MESH,
        )

    def send_pool(i):
        peer = sample_peer(i + 1)
        pool_copy(peer, s, peer).start()

    each(samples - 1, send_pool)
    pooled_out[...] = pooled

    def take_pool(i):
        source = lax.rem(s + samples - 1 - i, samples)
        pool_copy(s, source, s).wait_recv()

    each(samples - 1, take_pool)
    user_feat = dot_nn(picks, pool_all[...].reshape(group, width)).astype(BF16)

    pre = dot_nn(user_feat, wh_v[:half, :]) + pre_item
    cross = dot_nn(user_feat, wc_v[:half, :]) + cross_item
    pre_sq = pre * pre
    tanh = jnp.tanh(pre * (GELU_A + (GELU_A * GELU_B) * pre_sq))
    gate = 0.5 + 0.5 * tanh
    hidden = (pre * gate).astype(BF16)
    slope = gate + (0.5 * pre) * (1.0 - tanh * tanh) * (GELU_A + (3.0 * GELU_A * GELU_B) * pre_sq)
    loads[4].wait()
    lifted = jnp.concatenate([user_feat, items], axis=1).astype(F32)
    summed = dot_nn(hidden, wb_v[...]) + lifted * cross
    columns = 2 * width
    row_mean = jnp.sum(summed, axis=1, keepdims=True) * (1.0 / columns)
    centred = summed - row_mean
    row_var = jnp.sum(centred * centred, axis=1, keepdims=True) * (1.0 / columns)
    rstd = lax.rsqrt(row_var + 1e-05)
    raw_score = jnp.sum(centred * v_row, axis=1, keepdims=True)
    score = raw_score * rstd
    score_grad = jax.nn.sigmoid(score) - label_col
    pull = score_grad * rstd
    d_sum = pull * v_centred - centred * (pull * rstd * score * (1.0 / columns))
    d_hidden = dot_nt(d_sum.astype(BF16), wb_v[...]).astype(BF16).astype(F32)
    d_pre = (d_hidden * slope).astype(BF16)
    d_cross = (d_sum * lifted).astype(BF16)
    d_lift = d_sum * cross

    user_part = (
        d_lift[:, :half] + dot_nt(d_pre, wh_v[:half, :]) + dot_nt(d_cross, wc_v[:half, :])
    )
    per_user = dot_nn(picks_t, user_part.astype(BF16))
    grad_send[...] = per_user.astype(BF16).reshape(samples, users, width)

    def grad_copy(dst_sample, owner, src_sample):
        return pltpu.make_async_remote_copy(
            src_ref=grad_send.at[src_sample],
            dst_ref=grad_recv.at[owner],
            send_sem=grad_ssem.at[src_sample],
            recv_sem=grad_rsem.at[owner],
            device_id=(t, dst_sample),
            device_id_type=MESH,
        )

    def send_grad(i):
        peer = sample_peer(i + 1)
        grad_copy(peer, s, peer).start()

    each(samples - 1, send_grad)
    grad_recv[s] = grad_send[s]

    igrad_v[...] = (
        d_lift[:, half:] + dot_nt(d_pre, wh_v[half:, :]) + dot_nt(d_cross, wc_v[half:, :])
    )
    store = pltpu.make_async_copy(igrad_v, igrad_hbm, load_sem.at[5])
    store.start()
    scores_out[...] = jnp.transpose(jnp.broadcast_to(score, (imps, LANES)))[:1, :]

    def take_grad(i):
        source = lax.rem(s + samples - 1 - i, samples)
        grad_copy(s, source, s).wait_recv()

    each(samples - 1, take_grad)
    ugrad_out[...] = jnp.sum(grad_recv[...].astype(F32), axis=0)

    def sent_table(i):
        peer = table_peer(i + 1)
        ids_copy(peer, t, peer).wait_send()
        part_copy(peer, t, peer).wait_send()

    def sent_sample(i):
        peer = sample_peer(i + 1)
        pool_copy(peer, s, peer).wait_send()
        grad_copy(peer, s, peer).wait_send()

    each(tables - 1, sent_table)
    each(samples - 1, sent_sample)
    store.wait()


def body(tables, samples, *args):
    (
        hist_ids,
        hist_lens,
        table_rows,
        imp_user,
        item_rows,
        labels,
        w_hidden,
        b_hidden,
        w_back,
        w_cross,
        b_cross,
        norm_gain,
        w_score,
    ) = args
    users, _, slots = hist_ids.shape
    rows, width = table_rows.shape
    imps = item_rows.shape[0]
    history = slots * tables * 2 // 3
    assert (users * slots) % LANES == 0 and rows % LANES == 0 and users % 16 == 0
    chunks = -(-(users * slots // LANES) // 8) * 8
    vmem = pl.BlockSpec(memory_space=pltpu.VMEM)
    hbm = pl.BlockSpec(memory_space=pl.ANY)
    dma = pltpu.SemaphoreType.DMA

    def rowed(a):
        return a.reshape(1, -1)

    pooled, scores, user_grad, item_grad = pl.pallas_call(
        functools.partial(kernel, float(history) ** (-0.5)),
        out_shape=(
            jax.ShapeDtypeStruct((users, width), BF16),
            jax.ShapeDtypeStruct((1, imps), F32),
            jax.ShapeDtypeStruct((users, width), F32),
            jax.ShapeDtypeStruct((imps, width), F32),
        ),
        in_specs=[vmem, vmem, hbm, vmem, hbm, vmem, hbm, vmem, hbm, hbm, vmem, vmem, vmem],
        out_specs=(vmem, vmem, vmem, hbm),
        scratch_shapes=[
            pltpu.VMEM(table_rows.shape, BF16),
            pltpu.VMEM(item_rows.shape, BF16),
            pltpu.VMEM(w_hidden.shape, BF16),
            pltpu.VMEM(w_back.shape, BF16),
            pltpu.VMEM(w_cross.shape, BF16),
            pltpu.VMEM((tables, chunks, LANES), jnp.int32),
            pltpu.VMEM((tables, chunks, LANES), jnp.int32),
            pltpu.VMEM((tables * users, rows), BF16),
            pltpu.VMEM((tables, users, width), BF16),
            pltpu.VMEM((tables, users, width), BF16),
            pltpu.VMEM((samples, users, width), BF16),
            pltpu.VMEM((samples, users, width), BF16),
            pltpu.VMEM((samples, users, width), BF16),
            pltpu.VMEM((imps, width), F32),
            dma((6,)),
            dma((tables,)),
            dma((tables,)),
            dma((tables,)),
            dma((tables,)),
            dma((samples,)),
            dma((samples,)),
            dma((samples,)),
            dma((samples,)),
        ],
        compiler_params=pltpu.CompilerParams(
            collective_id=0, has_side_effects=True, vmem_limit_bytes=48 * 1024 * 1024
        ),
        cost_estimate=pl.CostEstimate(
            flops=1_500_000_000, bytes_accessed=4_000_000, transcendentals=200_000
        ),
    )(
        hist_ids,
        hist_lens,
        table_rows,
        rowed(imp_user),
        item_rows,
        rowed(labels),
        w_hidden,
        rowed(b_hidden),
        w_back,
        w_cross,
        rowed(b_cross),
        rowed(norm_gain),
        rowed(w_score),
    )
    return pooled, scores.reshape(imps), user_grad, item_grad


def solution(mesh):
    in_specs = (
        P(("table", "sample"), None, None),
        P(("table", "sample"), None),
        P("table", None),
        P(("table", "sample")),
        P(("table", "sample"), None),
        P(("table", "sample")),
        P(),
        P(),
        P(),
        P(),
        P(),
        P(),
        P(),
    )
    out_specs = (
        P(("table", "sample"), None),
        P(("table", "sample")),
        P(("table", "sample"), None),
        P(("table", "sample"), None),
    )
    step = functools.partial(body, mesh.shape["table"], mesh.shape["sample"])
    return jax.shard_map(step, mesh=mesh, in_specs=in_specs, out_specs=out_specs, check_vma=False)
```

time: 96.6 us -> 34.7 us (0.36)
  waiting for transfers between devices: 30.3 us -> 0 us
  Pallas kernels: 0 us -> 23.7 us
  other arithmetic: 15.1 us -> 0 us
  between operations: 14.3 us -> 0.68 us
  blocking collectives: 13.4 us -> 0 us
  starting transfers between devices: 12.2 us -> 0 us
  matrix products: 7.13 us -> 0 us
  local copies, waits for them, and re-layouts: 3.66 us -> 9.98 us
    pallas_call x0 -> x1, Pallas kernels: none -> 23.7 us  [body(): pl.pallas_call(functools.partial(kernel, float(history) ** (-0.5)), out_s...]
    reduce_scatter x1 -> x0, waiting for transfers between devices: 17.4 us -> none  [body(): lax.psum_scatter(per_user.astype(jnp.bfloat16), 'sample', scatter_dimensi...]
    all_gather x1 -> x0, blocking collectives: 13.4 us -> none  [body(): shard_part = lax.all_gather(pooled_user, 'sample', axis=0, tiled=True)]
    all_to_all x3 -> x0, waiting for transfers between devices: 13 us -> none  [the longest x1 5.3 us: body(): lax.all_to_all(partials, 'table', split_axis=1, concat_axis=1, tiled=True)]
    reduce_sum x5 -> x0, other arithmetic: 12.9 us -> none  [the longest x1 12.3 us: pool_block(): jnp.sum((masked_ids[:, :, None] == row_iota).astype(jnp.float32), axis=1)]
    all_to_all x3 -> x0, starting transfers between devices: 12.2 us -> none  [the longest x1 5.31 us: body(): lax.all_to_all(hist_lens, 'table', split_axis=1, concat_axis=1, tiled=True)]
    dot_general x9 -> x0, matrix products: 7.13 us -> none  [the longest x2 2.47 us: forward(): jnp.dot(joined, w_hidden, preferred_element_type=jnp.float32) + b_hidden]
    unnamed x31, local copies, waits for them, and re-layouts: 3.07 us -> 9.98 us
  transfers between devices with their start and end apart: 4 -> 0, of which waited for: 4 -> 0; matrix products, arithmetic and copies ran while one was open for 3% -> 0% of each run, Pallas kernels for 0% -> 0%
where the time goes in v1:
time: 34.7 us; the launch traced here: 34.3 us
  Pallas kernels  23.7 us (68%)
  local copies, waits for them, and re-layouts  9.98 us (29%)
  between operations  0.68 us (2%)
    pallas_call x1, Pallas kernels, body(): pl.pallas_call(functools.partial(kernel, float(history) ** (-0.5)), out_s...  23.7 us
    unnamed x31, local copies, waits for them, and re-layouts  9.98 us

profile of v1, /device:TPU:0, one launch (start us, length us, event | category | flops | bytes accessed | tf_op | source)
XLA Modules:
  0.0 34.3 jit_solution(14910118893330178568)
XLA Ops:
  0.6 0.0 copy-start.12
  0.6 0.7 %copy-done.12 = s32[16,8]{0,1:T(8,128)S(1)} copy-done((s32[16,8]{0,1:T(8,128)S(1)}, s32[16,8]{0,1:T(8,128)}, u32[]{:S(2)}) %copy-start.12) | copy-done | bytes 536
  1.3 0.0 copy-start.6
  1.3 0.0 copy-start.7
  1.3 0.0 copy-start.8
  1.3 0.0 copy-start.9
  1.3 0.0 copy-start.10
  1.3 0.0 copy-start.11
  1.4 0.1 copy.17.lens_ref
  1.4 0.6 %copy-done.6 = f32[512]{0:T(512)S(1)} copy-done((f32[512]{0:T(512)S(1)}, f32[512]{0:T(512)}, u32[]{:S(2)}) %copy-start.6) | copy-done | bytes 2072
  2.0 0.0 copy-done.7
  2.0 0.0 copy-done.8
  2.0 0.0 copy-done.9
  2.1 0.0 copy-done.10
  2.1 0.0 copy-done.11
  2.1 0.0 copy-start
  2.1 1.2 %copy-done = bf16[2048,256]{1,0:T(8,128)(2,1)S(1)} copy-done((bf16[2048,256]{1,0:T(8,128)(2,1)S(1)}, bf16[2048,256]{1,0:T(8,128)(2,1)}, u32[]{:S(2)}) %copy-start) | copy-done | bytes 1048600
  3.3 0.0 copy-start.1
  3.3 1.0 %copy-done.1 = bf16[512,512]{1,0:T(8,128)(2,1)S(1)} copy-done((bf16[512,512]{1,0:T(8,128)(2,1)S(1)}, bf16[512,512]{1,0:T(8,128)(2,1)}, u32[]{:S(2)}) %copy-start.1) | copy-done | bytes 524312
  4.3 0.0 copy-start.2
  4.3 1.0 %copy-done.2 = bf16[512,512]{1,0:T(8,128)(2,1)S(1)} copy-done((bf16[512,512]{1,0:T(8,128)(2,1)S(1)}, bf16[512,512]{1,0:T(8,128)(2,1)}, u32[]{:S(2)}) %copy-start.2) | copy-done | bytes 524312
  5.4 0.0 copy-start.3
  5.4 1.0 %copy-done.3 = bf16[512,512]{1,0:T(8,128)(2,1)S(1)} copy-done((bf16[512,512]{1,0:T(8,128)(2,1)S(1)}, bf16[512,512]{1,0:T(8,128)(2,1)}, u32[]{:S(2)}) %copy-start.3) | copy-done | bytes 524312
  6.4 0.0 copy-start.4
  6.4 0.9 %copy-done.4 = bf16[256,256]{1,0:T(8,128)(2,1)S(1)} copy-done((bf16[256,256]{1,0:T(8,128)(2,1)S(1)}, bf16[256,256]{1,0:T(8,128)(2,1)}, u32[]{:S(2)}) %copy-start.4) | copy-done | bytes 131096
  7.3 0.0 copy-start.5
  7.3 0.8 %copy-done.5 = s32[16,8,48]{2,1,0:T(8,128)S(1)} copy-done((s32[16,8,48]{2,1,0:T(8,128)S(1)}, s32[16,8,48]{2,1,0:T(8,128)}, u32[]{:S(2)}) %copy-start.5) | copy-done | bytes 24600
  8.2 23.7 %shard_map.156 = (bf16[16,256]{1,0:T(8,128)(2,1)S(1)}, f32[1,256]{1,0:T(1,128)S(1)}, f32[16,256]{1,0:T(8,128)S(1)}, f32[256,256]{1,0:T(8,128)S(1)}) custom-call(s32[16,8,48]{2,1,0:T(8,128)S(1)} %copy-done.5, s32[16,8]{1,0:T(8,128)S(1)} %copy.17.lens_ref, bf16[2048,256]{1,0:T(8,128)(2,1)S(1)} %copy-done, s32[1,256]{1,0:T(1,128)S(1)} %bitcast.12, ...), custom_call_target="tpu_custom_call" | custom-call | flops 1500000000 | bytes 4000000 | tf_op jit(solution)/shard_map/pallas_call | solution.py:381
  31.8 0.6 %copy.22 = bf16[16,256]{1,0:T(8,128)(2,1)} copy(bf16[16,256]{1,0:T(8,128)(2,1)S(1)} %get-tuple-element.16) | data formatting | bytes 16384
  32.4 0.6 %copy.23 = f32[256]{0:T(256)} copy(f32[256]{0:T(256)S(1)} %bitcast.7) | data formatting | bytes 2048
  33.0 0.6 %copy.24 = f32[16,256]{1,0:T(8,128)} copy(f32[16,256]{1,0:T(8,128)S(1)} %get-tuple-element.18) | data formatting | bytes 32768
  33.6 0.7 %copy.25 = f32[256,256]{1,0:T(8,128)} copy(f32[256,256]{1,0:T(8,128)S(1)} %get-tuple-element.19) | data formatting | bytes 524288
Async XLA Ops:
  0.6 0.7 %copy-start.12 = (s32[16,8]{0,1:T(8,128)S(1)}, s32[16,8]{0,1:T(8,128)}, u32[]{:S(2)}) copy-start(s32[16,8]{0,1:T(8,128)} %param.14) | copy-start | bytes 1540
  1.3 0.7 %copy-start.6 = (f32[512]{0:T(512)S(1)}, f32[512]{0:T(512)}, u32[]{:S(2)}) copy-start(f32[512]{0:T(512)} %param.20) | copy-start | bytes 6148
  1.3 0.7 %copy-start.7 = (f32[512]{0:T(512)S(1)}, f32[512]{0:T(512)}, u32[]{:S(2)}) copy-start(f32[512]{0:T(512)} %param.23) | copy-start | bytes 6148
  1.3 0.7 %copy-start.8 = (f32[512]{0:T(512)S(1)}, f32[512]{0:T(512)}, u32[]{:S(2)}) copy-start(f32[512]{0:T(512)} %param.24) | copy-start | bytes 6148
  1.3 0.7 %copy-start.9 = (f32[512]{0:T(512)S(1)}, f32[512]{0:T(512)}, u32[]{:S(2)}) copy-start(f32[512]{0:T(512)} %param.25) | copy-start | bytes 6148
  1.3 0.7 %copy-start.10 = (s32[256]{0:T(256)S(1)}, s32[256]{0:T(256)}, u32[]{:S(2)}) copy-start(s32[256]{0:T(256)} %param.16) | copy-start | bytes 3076
  1.3 0.7 %copy-start.11 = (s32[256]{0:T(256)S(1)}, s32[256]{0:T(256)}, u32[]{:S(2)}) copy-start(s32[256]{0:T(256)} %param.18) | copy-start | bytes 3076
  2.1 1.2 %copy-start = (bf16[2048,256]{1,0:T(8,128)(2,1)S(1)}, bf16[2048,256]{1,0:T(8,128)(2,1)}, u32[]{:S(2)}) copy-start(bf16[2048,256]{1,0:T(8,128)(2,1)} %table_hbm.1) | copy-start | bytes 3145732
  3.3 1.0 %copy-start.1 = (bf16[512,512]{1,0:T(8,128)(2,1)S(1)}, bf16[512,512]{1,0:T(8,128)(2,1)}, u32[]{:S(2)}) copy-start(bf16[512,512]{1,0:T(8,128)(2,1)} %wh_hbm.1) | copy-start | bytes 1572868
  4.3 1.0 %copy-start.2 = (bf16[512,512]{1,0:T(8,128)(2,1)S(1)}, bf16[512,512]{1,0:T(8,128)(2,1)}, u32[]{:S(2)}) copy-start(bf16[512,512]{1,0:T(8,128)(2,1)} %wb_hbm.1) | copy-start | bytes 1572868
  5.4 1.0 %copy-start.3 = (bf16[512,512]{1,0:T(8,128)(2,1)S(1)}, bf16[512,512]{1,0:T(8,128)(2,1)}, u32[]{:S(2)}) copy-start(bf16[512,512]{1,0:T(8,128)(2,1)} %wc_hbm.1) | copy-start | bytes 1572868
  6.4 0.9 %copy-start.4 = (bf16[256,256]{1,0:T(8,128)(2,1)S(1)}, bf16[256,256]{1,0:T(8,128)(2,1)}, u32[]{:S(2)}) copy-start(bf16[256,256]{1,0:T(8,128)(2,1)} %item_hbm.1) | copy-start | bytes 393220
  7.3 0.8 %copy-start.5 = (s32[16,8,48]{2,1,0:T(8,128)S(1)}, s32[16,8,48]{2,1,0:T(8,128)}, u32[]{:S(2)}) copy-start(s32[16,8,48]{2,1,0:T(8,128)} %ids_ref.1) | copy-start | bytes 73732

commit v2 on v1

--- a/solution.py
+++ b/solution.py
@@ -11,6 +11,7 @@
 F32 = jnp.float32
 BF16 = jnp.bfloat16
 LANES = 128
+VMEM_GRANT = 63 * 1024 * 1024
 GELU_A = 0.7978845608028654
 GELU_B = 0.044715
 
@@ -37,28 +38,36 @@
 
 def kernel(
     scale,
+    ids_hbm,
+    lens_hbm,
+    table_hbm,
+    imp_hbm,
+    item_hbm,
+    label_hbm,
+    wh_hbm,
+    bh_hbm,
+    wb_hbm,
+    wc_hbm,
+    bc_hbm,
+    gain_hbm,
+    ws_hbm,
+    pooled_out,
+    scores_out,
+    ugrad_out,
+    igrad_out,
     ids_ref,
     lens_ref,
-    table_hbm,
+    table_v,
     imp_ref,
-    item_hbm,
+    item_v,
     label_ref,
-    wh_hbm,
+    wh_v,
     bh_ref,
-    wb_hbm,
-    wc_hbm,
+    wb_v,
+    wc_v,
     bc_ref,
     gain_ref,
     ws_ref,
-    pooled_out,
-    scores_out,
-    ugrad_out,
-    igrad_hbm,
-    table_v,
-    item_v,
-    wh_v,
-    wb_v,
-    wc_v,
     msg,
     got,
     counts,
@@ -68,7 +77,10 @@
     grad_send,
     grad_recv,
     igrad_v,
+    scores_v,
+    ugrad_v,
     load_sem,
+    store_sem,
     ids_ssem,
     ids_rsem,
     part_ssem,
@@ -105,30 +117,37 @@
     each(tables - 1, greet_table)
     each(samples - 1, greet_sample)
 
-    loads = [
-        pltpu.make_async_copy(src, dst, load_sem.at[i])
-        for i, (src, dst) in enumerate(
-            [
-                (table_hbm, table_v),
-                (item_hbm, item_v),
-                (wh_hbm, wh_v),
-                (wc_hbm, wc_v),
-                (wb_hbm, wb_v),
-            ]
-        )
-    ]
-    for load in loads:
+    pairs = dict(
+        ids=(ids_hbm, ids_ref),
+        lens=(lens_hbm, lens_ref),
+        imp=(imp_hbm, imp_ref),
+        label=(label_hbm, label_ref),
+        gain=(gain_hbm, gain_ref),
+        ws=(ws_hbm, ws_ref),
+        table=(table_hbm, table_v),
+        item=(item_hbm, item_v),
+        bh=(bh_hbm, bh_ref),
+        bc=(bc_hbm, bc_ref),
+        wh=(wh_hbm, wh_v),
+        wc=(wc_hbm, wc_v),
+        wb=(wb_hbm, wb_v),
+    )
+    loads = {
+        name: pltpu.make_async_copy(src, dst, load_sem.at[i])
+        for i, (name, (src, dst)) in enumerate(pairs.items())
+    }
+    for load in loads.values():
         load.start()
 
-    eye = lax.broadcasted_iota(jnp.int32, (tables, tables), 0) == lax.broadcasted_iota(
-        jnp.int32, (tables, tables), 1
-    )
+    def arrived(*names):
+        for name in names:
+            loads[name].wait()
+
+    arrived("ids", "lens")
     slot_iota = lax.broadcasted_iota(jnp.int32, (tables, slots), 1)
     pieces = []
     for u in range(users):
-        lens_u = jnp.broadcast_to(lens_ref[u : u + 1, :], (tables, tables))
-        len_col = jnp.sum(jnp.where(eye, lens_u, 0), axis=1, keepdims=True)
-        pieces.append(jnp.where(slot_iota < len_col, ids_ref[u], -1))
+        pieces.append(jnp.where(slot_iota < lens_ref[:, u : u + 1], ids_ref[u], -1))
     packed = jnp.concatenate(pieces, axis=1)
     for c in range(users * slots // LANES):
         msg[:, c, :] = packed[:, c * LANES : (c + 1) * LANES]
@@ -154,6 +173,7 @@
     each(tables - 1, send_ids)
     got[t] = msg[t]
 
+    arrived("imp", "label", "gain", "ws")
     imp_row = imp_ref[...].astype(F32)
     imp_col = to_column(imp_row, LANES)[:, :1]
     picks = jnp.where(
@@ -173,8 +193,9 @@
     user_of = jnp.zeros((chunks, LANES), jnp.int32)
     for u in range(1, users):
         user_of = user_of + jnp.where(position >= u * slots, 1, 0)
-    hi_iota = lax.broadcasted_iota(jnp.int32, (n_hi * users, LANES), 0)
-    lo_iota = lax.broadcasted_iota(jnp.int32, (LANES, LANES), 0)
+    hi_iota = lax.broadcasted_iota(jnp.int32, (n_hi * users, LANES), 0).astype(F32).astype(BF16)
+    lo_iota = hi_iota[:LANES]
+    one, zero = jnp.ones((), BF16), jnp.zeros((), BF16)
     used = users * slots // LANES
 
     def count_source(i):
@@ -189,12 +210,12 @@
                 ids_copy(t, source, t).wait_recv()
 
         ids = got[source]
-        hi_key = jnp.where(ids >= 0, (ids >> 7) * users + user_of, -1)
-        lo_key = ids & (LANES - 1)
+        hi_key = jnp.where(ids >= 0, (ids >> 7) * users + user_of, -1).astype(F32).astype(BF16)
+        lo_key = (ids & (LANES - 1)).astype(F32).astype(BF16)
         hi_hot, lo_hot = [], []
         for c in range(used):
-            hi_hot.append(jnp.where(hi_key[c : c + 1, :] == hi_iota, 1.0, 0.0).astype(BF16))
-            lo_hot.append(jnp.where(lo_key[c : c + 1, :] == lo_iota, 1.0, 0.0).astype(BF16))
+            hi_hot.append(jnp.where(hi_key[c : c + 1, :] == hi_iota, one, zero))
+            lo_hot.append(jnp.where(lo_key[c : c + 1, :] == lo_iota, one, zero))
         block = dot_nt(jnp.concatenate(hi_hot, axis=1), jnp.concatenate(lo_hot, axis=1))
         block = block.astype(BF16)
         rows = pl.ds(pl.multiple_of(source * users, users), users)
@@ -203,7 +224,7 @@
 
     each(tables, count_source)
 
-    loads[0].wait()
+    arrived("table")
     per_step = min(tables, 8)
     table_all = table_v[...]
 
@@ -231,9 +252,7 @@
     each(tables - 1, send_part)
     part_recv[t] = part_send[t]
 
-    loads[1].wait()
-    loads[2].wait()
-    loads[3].wait()
+    arrived("item", "wh", "wc", "bh", "bc")
     items = item_v[...]
     half = width
     pre_item = dot_nn(items, wh_v[half:, :]) + bh_ref[...]
@@ -263,7 +282,8 @@
         pool_copy(peer, s, peer).start()
 
     each(samples - 1, send_pool)
-    pooled_out[...] = pooled
+    stores = [pltpu.make_async_copy(pool_all.at[s], pooled_out, store_sem.at[0])]
+    stores[0].start()
 
     def take_pool(i):
         source = lax.rem(s + samples - 1 - i, samples)
@@ -279,7 +299,7 @@
     gate = 0.5 + 0.5 * tanh
     hidden = (pre * gate).astype(BF16)
     slope = gate + (0.5 * pre) * (1.0 - tanh * tanh) * (GELU_A + (3.0 * GELU_A * GELU_B) * pre_sq)
-    loads[4].wait()
+    arrived("wb")
     lifted = jnp.concatenate([user_feat, items], axis=1).astype(F32)
     summed = dot_nn(hidden, wb_v[...]) + lifted * cross
     columns = 2 * width
@@ -323,16 +343,20 @@
     igrad_v[...] = (
         d_lift[:, half:] + dot_nt(d_pre, wh_v[half:, :]) + dot_nt(d_cross, wc_v[half:, :])
     )
-    store = pltpu.make_async_copy(igrad_v, igrad_hbm, load_sem.at[5])
-    store.start()
-    scores_out[...] = jnp.transpose(jnp.broadcast_to(score, (imps, LANES)))[:1, :]
+    stores.append(pltpu.make_async_copy(igrad_v, igrad_out, store_sem.at[1]))
+    stores[1].start()
+    scores_v[...] = jnp.transpose(jnp.broadcast_to(score, (imps, LANES)))[:1, :]
+    stores.append(pltpu.make_async_copy(scores_v, scores_out, store_sem.at[2]))
+    stores[2].start()
 
     def take_grad(i):
         source = lax.rem(s + samples - 1 - i, samples)
         grad_copy(s, source, s).wait_recv()
 
     each(samples - 1, take_grad)
-    ugrad_out[...] = jnp.sum(grad_recv[...].astype(F32), axis=0)
+    ugrad_v[...] = jnp.sum(grad_recv[...].astype(F32), axis=0)
+    stores.append(pltpu.make_async_copy(ugrad_v, ugrad_out, store_sem.at[3]))
+    stores[3].start()
 
     def sent_table(i):
         peer = table_peer(i + 1)
@@ -346,7 +370,23 @@
 
     each(tables - 1, sent_table)
     each(samples - 1, sent_sample)
-    store.wait()
+    for store in stores:
+        store.wait()
+
+
+def write_out(*refs):
+    *arrays, sems = refs
+    count = len(arrays) // 2
+    jobs = []
+    for src, dst in zip(arrays[:count], arrays[count:]):
+        parts = 4 if src.shape[0] % 64 == 0 else 1
+        rows = src.shape[0] // parts
+        jobs += [(src.at[pl.ds(k * rows, rows)], dst.at[pl.ds(k * rows, rows)]) for k in range(parts)]
+    copies = [pltpu.make_async_copy(*job, sems.at[i]) for i, job in enumerate(jobs)]
+    for copy in copies:
+        copy.start()
+    for copy in copies:
+        copy.wait()
 
 
 def body(tables, samples, *args):
@@ -371,57 +411,15 @@
     history = slots * tables * 2 // 3
     assert (users * slots) % LANES == 0 and rows % LANES == 0 and users % 16 == 0
     chunks = -(-(users * slots // LANES) // 8) * 8
-    vmem = pl.BlockSpec(memory_space=pltpu.VMEM)
-    hbm = pl.BlockSpec(memory_space=pl.ANY)
+    hbm = pl.BlockSpec(memory_space=pltpu.HBM)
     dma = pltpu.SemaphoreType.DMA
 
     def rowed(a):
         return a.reshape(1, -1)
 
-    pooled, scores, user_grad, item_grad = pl.pallas_call(
-        functools.partial(kernel, float(history) ** (-0.5)),
-        out_shape=(
-            jax.ShapeDtypeStruct((users, width), BF16),
-            jax.ShapeDtypeStruct((1, imps), F32),
-            jax.ShapeDtypeStruct((users, width), F32),
-            jax.ShapeDtypeStruct((imps, width), F32),
-        ),
-        in_specs=[vmem, vmem, hbm, vmem, hbm, vmem, hbm, vmem, hbm, hbm, vmem, vmem, vmem],
-        out_specs=(vmem, vmem, vmem, hbm),
-        scratch_shapes=[
-            pltpu.VMEM(table_rows.shape, BF16),
-            pltpu.VMEM(item_rows.shape, BF16),
-            pltpu.VMEM(w_hidden.shape, BF16),
-            pltpu.VMEM(w_back.shape, BF16),
-            pltpu.VMEM(w_cross.shape, BF16),
-            pltpu.VMEM((tables, chunks, LANES), jnp.int32),
-            pltpu.VMEM((tables, chunks, LANES), jnp.int32),
-            pltpu.VMEM((tables * users, rows), BF16),
-            pltpu.VMEM((tables, users, width), BF16),
-            pltpu.VMEM((tables, users, width), BF16),
-            pltpu.VMEM((samples, users, width), BF16),
-            pltpu.VMEM((samples, users, width), BF16),
-            pltpu.VMEM((samples, users, width), BF16),
-            pltpu.VMEM((imps, width), F32),
-            dma((6,)),
-            dma((tables,)),
-            dma((tables,)),
-            dma((tables,)),
-            dma((tables,)),
-            dma((samples,)),
-            dma((samples,)),
-            dma((samples,)),
-            dma((samples,)),
-        ],
-        compiler_params=pltpu.CompilerParams(
-            collective_id=0, has_side_effects=True, vmem_limit_bytes=48 * 1024 * 1024
-        ),
-        cost_estimate=pl.CostEstimate(
-            flops=1_500_000_000, bytes_accessed=4_000_000, transcendentals=200_000
-        ),
-    )(
+    operands = (
         hist_ids,
-        hist_lens,
+        hist_lens.T,
         table_rows,
         rowed(imp_user),
         item_rows,
@@ -434,6 +432,56 @@
         rowed(norm_gain),
         rowed(w_score),
     )
+    shapes = (
+        jax.ShapeDtypeStruct((users, width), BF16),
+        jax.ShapeDtypeStruct((1, imps), F32),
+        jax.ShapeDtypeStruct((users, width), F32),
+        jax.ShapeDtypeStruct((imps, width), F32),
+    )
+    results = pl.pallas_call(
+        functools.partial(kernel, float(history) ** (-0.5)),
+        out_shape=shapes,
+        in_specs=[hbm] * len(operands),
+        out_specs=(hbm,) * len(shapes),
+        scratch_shapes=[
+            *[pltpu.VMEM(a.shape, a.dtype) for a in operands],
+            pltpu.VMEM((tables, chunks, LANES), jnp.int32),
+            pltpu.VMEM((tables, chunks, LANES), jnp.int32),
+            pltpu.VMEM((tables * users, rows), BF16),
+            pltpu.VMEM((tables, users, width), BF16),
+            pltpu.VMEM((tables, users, width), BF16),
+            pltpu.VMEM((samples, users, width), BF16),
+            pltpu.VMEM((samples, users, width), BF16),
+            pltpu.VMEM((samples, users, width), BF16),
+            pltpu.VMEM((imps, width), F32),
+            pltpu.VMEM((1, imps), F32),
+            pltpu.VMEM((users, width), F32),
+            dma((len(operands),)),
+            dma((len(shapes),)),
+            dma((tables,)),
+            dma((tables,)),
+            dma((tables,)),
+            dma((tables,)),
+            dma((samples,)),
+            dma((samples,)),
+            dma((samples,)),
+            dma((samples,)),
+        ],
+        compiler_params=pltpu.CompilerParams(
+            collective_id=0, has_side_effects=True, vmem_limit_bytes=VMEM_GRANT
+        ),
+        cost_estimate=pl.CostEstimate(
+            flops=1_500_000_000, bytes_accessed=4_000_000, transcendentals=200_000
+        ),
+    )(*operands)
+    pooled, scores, user_grad, item_grad = pl.pallas_call(
+        write_out,
+        out_shape=shapes,
+        in_specs=[hbm] * len(shapes),
+        out_specs=(hbm,) * len(shapes),
+        scratch_shapes=[dma((4 * len(shapes),))],
+        compiler_params=pltpu.CompilerParams(vmem_limit_bytes=VMEM_GRANT),
+    )(*results)
     return pooled, scores.reshape(imps), user_grad, item_grad
 
 

time: 34.7 us -> 35.2 us (1.014)
  Pallas kernels: 23.7 us -> 34.4 us
  local copies, waits for them, and re-layouts: 9.98 us -> 0 us
    unnamed x31 -> x0, local copies, waits for them, and re-layouts: 9.98 us -> none
    pallas_call x0 -> x1, Pallas kernels: none -> 9.96 us  [body(): pl.pallas_call(write_out, out_shape=shapes, in_specs=[hbm] * len(shapes),...]
    pallas_call x1, Pallas kernels: 23.7 us -> 24.4 us  [body(): pl.pallas_call(functools.partial(kernel, float(history) ** (-0.5)), out_s...]
where the time goes in v2:
time: 35.2 us; the launch traced here: 35 us
  Pallas kernels  34.4 us (98%)
  between operations  0.64 us (2%)
    pallas_call x1, Pallas kernels, body(): pl.pallas_call(functools.partial(kernel, float(history) ** (-0.5)), out_s...  24.4 us
    pallas_call x1, Pallas kernels, body(): pl.pallas_call(write_out, out_shape=shapes, in_specs=[hbm] * len(shapes),...  9.96 us

profile of v2, /device:TPU:0, one launch (start us, length us, event | category | flops | bytes accessed | tf_op | source)
XLA Modules:
  0.0 35.0 jit_solution(12508320948345698025)
XLA Ops:
  0.6 24.4 %shard_map.156 = (bf16[16,256]{1,0:T(8,128)(2,1)}, f32[1,256]{1,0:T(1,128)}, f32[16,256]{1,0:T(8,128)}, f32[256,256]{1,0:T(8,128)}) custom-call(s32[16,8,48]{2,1,0:T(8,128)} %ids_hbm.1, s32[8,16]{1,0:T(8,128)} %bitcast.8, bf16[2048,256]{1,0:T(8,128)(2,1)} %table_hbm.1, s32[1,256]{1,0:T(1,128)} %bitcast.13, bf16[256,256]{1,0:T(8,128)(2,1)} %item_hbm.1, ...), custom_call_target="tpu_custom_call" | custom-call | flops 1500000000 | bytes 4000000 | tf_op jit(solution)/shard_map/pallas_call | solution.py:441
  25.1 10.0 %shard_map.157 = (bf16[16,256]{1,0:T(8,128)(2,1)}, f32[1,256]{1,0:T(1,128)}, f32[16,256]{1,0:T(8,128)}, f32[256,256]{1,0:T(8,128)}) custom-call(bf16[16,256]{1,0:T(8,128)(2,1)} %get-tuple-element.12.refs_0_, f32[1,256]{1,0:T(1,128)} %get-tuple-element.13.refs_1_, f32[16,256]{1,0:T(8,128)} %get-tuple-element.14.refs_2_, f32[256,256]{1,0:T(8,128)} %get-tuple-element.15.refs_3_), custom_call_target="tpu_custom_call" | custom-call | tf_op jit(solution)/shard_map/pallas_call | solution.py:477

commit v3 on v2

--- a/solution.py
+++ b/solution.py
@@ -26,6 +26,13 @@
 
 def to_column(row, width):
     return jnp.transpose(jnp.broadcast_to(row, (width, row.shape[1])))
+
+
+def by_rows(body, *arrays, rows=32):
+    total = arrays[0].shape[0]
+    step = rows if total % rows == 0 else total
+    blocks = [body(*[a[k : k + step] for a in arrays]) for k in range(0, total, step)]
+    return tuple(jnp.concatenate(parts, axis=0) for parts in zip(*blocks))
 
 
 def each(count, body):
@@ -106,17 +113,6 @@
     def sample_peer(d):
         return lax.rem(s + d, samples)
 
-    barrier = pltpu.get_barrier_semaphore()
-
-    def greet_table(i):
-        pl.semaphore_signal(barrier, inc=1, device_id=(table_peer(i + 1), s), device_id_type=MESH)
-
-    def greet_sample(i):
-        pl.semaphore_signal(barrier, inc=1, device_id=(t, sample_peer(i + 1)), device_id_type=MESH)
-
-    each(tables - 1, greet_table)
-    each(samples - 1, greet_sample)
-
     pairs = dict(
         ids=(ids_hbm, ids_ref),
         lens=(lens_hbm, lens_ref),
@@ -136,8 +132,23 @@
         name: pltpu.make_async_copy(src, dst, load_sem.at[i])
         for i, (name, (src, dst)) in enumerate(pairs.items())
     }
-    for load in loads.values():
-        load.start()
+    loads["ids"].start()
+    loads["lens"].start()
+
+    barrier = pltpu.get_barrier_semaphore()
+
+    def greet_table(i):
+        pl.semaphore_signal(barrier, inc=1, device_id=(table_peer(i + 1), s), device_id_type=MESH)
+
+    def greet_sample(i):
+        pl.semaphore_signal(barrier, inc=1, device_id=(t, sample_peer(i + 1)), device_id_type=MESH)
+
+    each(tables - 1, greet_table)
+    each(samples - 1, greet_sample)
+
+    for name, load in loads.items():
+        if name not in ("ids", "lens"):
+            load.start()
 
     def arrived(*names):
         for name in names:
@@ -292,30 +303,45 @@
     each(samples - 1, take_pool)
     user_feat = dot_nn(picks, pool_all[...].reshape(group, width)).astype(BF16)
 
-    pre = dot_nn(user_feat, wh_v[:half, :]) + pre_item
-    cross = dot_nn(user_feat, wc_v[:half, :]) + cross_item
-    pre_sq = pre * pre
-    tanh = jnp.tanh(pre * (GELU_A + (GELU_A * GELU_B) * pre_sq))
-    gate = 0.5 + 0.5 * tanh
-    hidden = (pre * gate).astype(BF16)
-    slope = gate + (0.5 * pre) * (1.0 - tanh * tanh) * (GELU_A + (3.0 * GELU_A * GELU_B) * pre_sq)
+    pre_all = dot_nn(user_feat, wh_v[:half, :])
+    cross_all = dot_nn(user_feat, wc_v[:half, :])
+    columns = 2 * width
+    lifted_all = jnp.concatenate([user_feat, items], axis=1)
+
+    def activate(pre, pre_add):
+        pre = pre + pre_add
+        pre_sq = pre * pre
+        tanh = jnp.tanh(pre * (GELU_A + (GELU_A * GELU_B) * pre_sq))
+        gate = 0.5 + 0.5 * tanh
+        rise = (0.5 * GELU_A) + (1.5 * GELU_A * GELU_B) * pre_sq
+        slope = gate + pre * (1.0 - tanh * tanh) * rise
+        return (pre * gate).astype(BF16), slope
+
+    hidden, slope_all = by_rows(activate, pre_all, pre_item)
     arrived("wb")
-    lifted = jnp.concatenate([user_feat, items], axis=1).astype(F32)
-    summed = dot_nn(hidden, wb_v[...]) + lifted * cross
-    columns = 2 * width
-    row_mean = jnp.sum(summed, axis=1, keepdims=True) * (1.0 / columns)
-    centred = summed - row_mean
-    row_var = jnp.sum(centred * centred, axis=1, keepdims=True) * (1.0 / columns)
-    rstd = lax.rsqrt(row_var + 1e-05)
-    raw_score = jnp.sum(centred * v_row, axis=1, keepdims=True)
-    score = raw_score * rstd
-    score_grad = jax.nn.sigmoid(score) - label_col
-    pull = score_grad * rstd
-    d_sum = pull * v_centred - centred * (pull * rstd * score * (1.0 / columns))
-    d_hidden = dot_nt(d_sum.astype(BF16), wb_v[...]).astype(BF16).astype(F32)
-    d_pre = (d_hidden * slope).astype(BF16)
-    d_cross = (d_sum * lifted).astype(BF16)
-    d_lift = d_sum * cross
+    back = dot_nn(hidden, wb_v[...])
+
+    def score_rows(back, cross, cross_add, lifted, label):
+        lifted = lifted.astype(F32)
+        cross = cross + cross_add
+        summed = back + lifted * cross
+        row_mean = jnp.sum(summed, axis=1, keepdims=True) * (1.0 / columns)
+        centred = summed - row_mean
+        row_var = jnp.sum(centred * centred, axis=1, keepdims=True) * (1.0 / columns)
+        raw_score = jnp.sum(centred * v_row, axis=1, keepdims=True)
+        rstd = lax.rsqrt(row_var + 1e-05)
+        score = raw_score * rstd
+        pull = (jax.nn.sigmoid(score) - label) * rstd
+        d_sum = pull * v_centred - centred * (pull * rstd * score * (1.0 / columns))
+        return score, d_sum.astype(BF16), (d_sum * lifted).astype(BF16), d_sum * cross
+
+    score, d_sum, d_cross, d_lift = by_rows(
+        score_rows, back, cross_all, cross_item, lifted_all, label_col
+    )
+    d_hidden = dot_nt(d_sum, wb_v[...])
+    (d_pre,) = by_rows(
+        lambda d, slope: ((d.astype(BF16).astype(F32) * slope).astype(BF16),), d_hidden, slope_all
+    )
 
     user_part = (
         d_lift[:, :half] + dot_nt(d_pre, wh_v[:half, :]) + dot_nt(d_cross, wc_v[:half, :])
@@ -376,17 +402,17 @@
 
 def write_out(*refs):
     *arrays, sems = refs
-    count = len(arrays) // 2
-    jobs = []
-    for src, dst in zip(arrays[:count], arrays[count:]):
-        parts = 4 if src.shape[0] % 64 == 0 else 1
-        rows = src.shape[0] // parts
-        jobs += [(src.at[pl.ds(k * rows, rows)], dst.at[pl.ds(k * rows, rows)]) for k in range(parts)]
-    copies = [pltpu.make_async_copy(*job, sems.at[i]) for i, job in enumerate(jobs)]
-    for copy in copies:
-        copy.start()
-    for copy in copies:
-        copy.wait()
+    count = len(arrays) // 3
+    sources, targets, held = arrays[:count], arrays[count : 2 * count], arrays[2 * count :]
+    loads = [pltpu.make_async_copy(sources[i], held[i], sems.at[0, i]) for i in range(count)]
+    stores = [pltpu.make_async_copy(held[i], targets[i], sems.at[1, i]) for i in range(count)]
+    for load in loads[::-1]:
+        load.start()
+    for load, store in zip(loads, stores):
+        load.wait()
+        store.start()
+    for store in stores:
+        store.wait()
 
 
 def body(tables, samples, *args):
@@ -479,7 +505,7 @@
         out_shape=shapes,
         in_specs=[hbm] * len(shapes),
         out_specs=(hbm,) * len(shapes),
-        scratch_shapes=[dma((4 * len(shapes),))],
+        scratch_shapes=[*[pltpu.VMEM(a.shape, a.dtype) for a in shapes], dma((2, len(shapes)))],
         compiler_params=pltpu.CompilerParams(vmem_limit_bytes=VMEM_GRANT),
     )(*results)
     return pooled, scores.reshape(imps), user_grad, item_grad

time: 35.2 us -> 26.9 us (0.76)
  Pallas kernels: 34.4 us -> 26.1 us
    pallas_call x1, Pallas kernels: 9.96 us -> 1.72 us  [body(): pl.pallas_call(write_out, out_shape=shapes, in_specs=[hbm] * len(shapes),...]
where the time goes in v3:
time: 26.9 us; the launch traced here: 26.8 us
  Pallas kernels  26.1 us (97%)
  between operations  0.64 us (2%)
    pallas_call x1, Pallas kernels, body(): pl.pallas_call(functools.partial(kernel, float(history) ** (-0.5)), out_s...  24.4 us
    pallas_call x1, Pallas kernels, body(): pl.pallas_call(write_out, out_shape=shapes, in_specs=[hbm] * len(shapes),...  1.72 us

profile of v3, /device:TPU:0, one launch (start us, length us, event | category | flops | bytes accessed | tf_op | source)
XLA Modules:
  0.0 26.8 jit_solution(15146298063521208929)
XLA Ops:
  0.6 24.4 %shard_map.156 = (bf16[16,256]{1,0:T(8,128)(2,1)}, f32[1,256]{1,0:T(1,128)}, f32[16,256]{1,0:T(8,128)}, f32[256,256]{1,0:T(8,128)}) custom-call(s32[16,8,48]{2,1,0:T(8,128)} %ids_hbm.1, s32[8,16]{1,0:T(8,128)} %bitcast.8, bf16[2048,256]{1,0:T(8,128)(2,1)} %table_hbm.1, s32[1,256]{1,0:T(1,128)} %bitcast.13, bf16[256,256]{1,0:T(8,128)(2,1)} %item_hbm.1, ...), custom_call_target="tpu_custom_call" | custom-call | flops 1500000000 | bytes 4000000 | tf_op jit(solution)/shard_map/pallas_call | solution.py:467
  25.1 1.7 %shard_map.157 = (bf16[16,256]{1,0:T(8,128)(2,1)}, f32[1,256]{1,0:T(1,128)}, f32[16,256]{1,0:T(8,128)}, f32[256,256]{1,0:T(8,128)}) custom-call(bf16[16,256]{1,0:T(8,128)(2,1)} %get-tuple-element.12.refs_0_, f32[1,256]{1,0:T(1,128)} %get-tuple-element.13.refs_1_, f32[16,256]{1,0:T(8,128)} %get-tuple-element.14.refs_2_, f32[256,256]{1,0:T(8,128)} %get-tuple-element.15.refs_3_), custom_call_target="tpu_custom_call" | custom-call | tf_op jit(solution)/shard_map/pallas_call | solution.py:503

commit v4 on v3

--- a/solution.py
+++ b/solution.py
@@ -86,6 +86,9 @@
     igrad_v,
     scores_v,
     ugrad_v,
+    wb_t,
+    wh_t,
+    wc_t,
     load_sem,
     store_sem,
     ids_ssem,
@@ -295,6 +298,10 @@
     each(samples - 1, send_pool)
     stores = [pltpu.make_async_copy(pool_all.at[s], pooled_out, store_sem.at[0])]
     stores[0].start()
+    arrived("wb")
+    wb_t[...] = jnp.transpose(wb_v[...])
+    wh_t[...] = jnp.transpose(wh_v[:half, :])
+    wc_t[...] = jnp.transpose(wc_v[:half, :])
 
     def take_pool(i):
         source = lax.rem(s + samples - 1 - i, samples)
@@ -318,7 +325,6 @@
         return (pre * gate).astype(BF16), slope
 
     hidden, slope_all = by_rows(activate, pre_all, pre_item)
-    arrived("wb")
     back = dot_nn(hidden, wb_v[...])
 
     def score_rows(back, cross, cross_add, lifted, label):
@@ -338,13 +344,13 @@
     score, d_sum, d_cross, d_lift = by_rows(
         score_rows, back, cross_all, cross_item, lifted_all, label_col
     )
-    d_hidden = dot_nt(d_sum, wb_v[...])
+    d_hidden = dot_nn(d_sum, wb_t[...])
     (d_pre,) = by_rows(
         lambda d, slope: ((d.astype(BF16).astype(F32) * slope).astype(BF16),), d_hidden, slope_all
     )
 
     user_part = (
-        d_lift[:, :half] + dot_nt(d_pre, wh_v[:half, :]) + dot_nt(d_cross, wc_v[:half, :])
+        d_lift[:, :half] + dot_nn(d_pre, wh_t[...]) + dot_nn(d_cross, wc_t[...])
     )
     per_user = dot_nn(picks_t, user_part.astype(BF16))
     grad_send[...] = per_user.astype(BF16).reshape(samples, users, width)
@@ -482,6 +488,9 @@
             pltpu.VMEM((imps, width), F32),
             pltpu.VMEM((1, imps), F32),
             pltpu.VMEM((users, width), F32),
+            pltpu.VMEM(w_back.shape[::-1], BF16),
+            pltpu.VMEM((w_hidden.shape[1], width), BF16),
+            pltpu.VMEM((w_cross.shape[1], width), BF16),
             dma((len(operands),)),
             dma((len(shapes),)),
             dma((tables,)),

time: 26.9 us -> 26.7 us (level)
    pallas_call x1, Pallas kernels: 24.4 us -> 24.1 us  [body(): pl.pallas_call(functools.partial(kernel, float(history) ** (-0.5)), out_s...]
where the time goes in v4:
time: 26.7 us; the launch traced here: 26.5 us
  Pallas kernels  25.9 us (97%)
  between operations  0.64 us (2%)
    pallas_call x1, Pallas kernels, body(): pl.pallas_call(functools.partial(kernel, float(history) ** (-0.5)), out_s...  24.1 us
    pallas_call x1, Pallas kernels, body(): pl.pallas_call(write_out, out_shape=shapes, in_specs=[hbm] * len(shapes),...  1.72 us

profile of v4, /device:TPU:0, one launch (start us, length us, event | category | flops | bytes accessed | tf_op | source)
XLA Modules:
  0.0 26.5 jit_solution(5608038778203683585)
XLA Ops:
  0.6 24.1 %shard_map.156 = (bf16[16,256]{1,0:T(8,128)(2,1)}, f32[1,256]{1,0:T(1,128)}, f32[16,256]{1,0:T(8,128)}, f32[256,256]{1,0:T(8,128)}) custom-call(s32[16,8,48]{2,1,0:T(8,128)} %ids_hbm.1, s32[8,16]{1,0:T(8,128)} %bitcast.8, bf16[2048,256]{1,0:T(8,128)(2,1)} %table_hbm.1, s32[1,256]{1,0:T(1,128)} %bitcast.13, bf16[256,256]{1,0:T(8,128)(2,1)} %item_hbm.1, ...), custom_call_target="tpu_custom_call" | custom-call | flops 1500000000 | bytes 4000000 | tf_op jit(solution)/shard_map/pallas_call | solution.py:473
  24.8 1.7 %shard_map.157 = (bf16[16,256]{1,0:T(8,128)(2,1)}, f32[1,256]{1,0:T(1,128)}, f32[16,256]{1,0:T(8,128)}, f32[256,256]{1,0:T(8,128)}) custom-call(bf16[16,256]{1,0:T(8,128)(2,1)} %get-tuple-element.12.refs_0_, f32[1,256]{1,0:T(1,128)} %get-tuple-element.13.refs_1_, f32[16,256]{1,0:T(8,128)} %get-tuple-element.14.refs_2_, f32[256,256]{1,0:T(8,128)} %get-tuple-element.15.refs_3_), custom_call_target="tpu_custom_call" | custom-call | tf_op jit(solution)/shard_map/pallas_call | solution.py:512

commit v5 on v4

--- a/solution.py
+++ b/solution.py
@@ -207,7 +207,8 @@
     user_of = jnp.zeros((chunks, LANES), jnp.int32)
     for u in range(1, users):
         user_of = user_of + jnp.where(position >= u * slots, 1, 0)
-    hi_iota = lax.broadcasted_iota(jnp.int32, (n_hi * users, LANES), 0).astype(F32).astype(BF16)
+    user_of = jnp.where(user_of >= users // 2, user_of - users // 2, user_of)
+    hi_iota = lax.broadcasted_iota(jnp.int32, (n_hi * users // 2, LANES), 0).astype(F32).astype(BF16)
     lo_iota = hi_iota[:LANES]
     one, zero = jnp.ones((), BF16), jnp.zeros((), BF16)
     used = users * slots // LANES
@@ -224,17 +225,25 @@
                 ids_copy(t, source, t).wait_recv()
 
         ids = got[source]
-        hi_key = jnp.where(ids >= 0, (ids >> 7) * users + user_of, -1).astype(F32).astype(BF16)
+        hi_key = jnp.where(ids >= 0, (ids >> 7) * (users // 2) + user_of, -1).astype(F32).astype(BF16)
         lo_key = (ids & (LANES - 1)).astype(F32).astype(BF16)
         hi_hot, lo_hot = [], []
         for c in range(used):
             hi_hot.append(jnp.where(hi_key[c : c + 1, :] == hi_iota, one, zero))
             lo_hot.append(jnp.where(lo_key[c : c + 1, :] == lo_iota, one, zero))
-        block = dot_nt(jnp.concatenate(hi_hot, axis=1), jnp.concatenate(lo_hot, axis=1))
-        block = block.astype(BF16)
+        few, cut = users // 2, used // 2
+        top, bottom = [
+            dot_nt(
+                jnp.concatenate(hi_hot[k : k + cut], axis=1),
+                jnp.concatenate(lo_hot[k : k + cut], axis=1),
+            )
+            for k in (0, cut)
+        ]
         rows = pl.ds(pl.multiple_of(source * users, users), users)
         for h in range(n_hi):
-            counts[rows, h * LANES : (h + 1) * LANES] = block[h * users : (h + 1) * users, :]
+            own = slice(h * few, (h + 1) * few)
+            both = jnp.concatenate([top[own], bottom[own]], axis=0)
+            counts[rows, h * LANES : (h + 1) * LANES] = both.astype(BF16)
 
     each(tables, count_source)
 
@@ -441,7 +450,7 @@
     rows, width = table_rows.shape
     imps = item_rows.shape[0]
     history = slots * tables * 2 // 3
-    assert (users * slots) % LANES == 0 and rows % LANES == 0 and users % 16 == 0
+    assert (users * slots) % (2 * LANES) == 0 and rows % LANES == 0 and users % 16 == 0
     chunks = -(-(users * slots // LANES) // 8) * 8
     hbm = pl.BlockSpec(memory_space=pltpu.HBM)
     dma = pltpu.SemaphoreType.DMA

time: 26.7 us -> 25.9 us (0.970)
  Pallas kernels: 25.9 us -> 25.1 us
    pallas_call x1, Pallas kernels: 24.1 us -> 23.4 us  [body(): pl.pallas_call(functools.partial(kernel, float(history) ** (-0.5)), out_s...]
where the time goes in v5:
time: 25.9 us; the launch traced here: 25.8 us
  Pallas kernels  25.1 us (97%)
  between operations  0.64 us (2%)
    pallas_call x1, Pallas kernels, body(): pl.pallas_call(functools.partial(kernel, float(history) ** (-0.5)), out_s...  23.4 us
    pallas_call x1, Pallas kernels, body(): pl.pallas_call(write_out, out_shape=shapes, in_specs=[hbm] * len(shapes),...  1.72 us

profile of v5, /device:TPU:0, one launch (start us, length us, event | category | flops | bytes accessed | tf_op | source)
XLA Modules:
  0.0 25.8 jit_solution(16193698267726459927)
XLA Ops:
  0.6 23.4 %shard_map.156 = (bf16[16,256]{1,0:T(8,128)(2,1)}, f32[1,256]{1,0:T(1,128)}, f32[16,256]{1,0:T(8,128)}, f32[256,256]{1,0:T(8,128)}) custom-call(s32[16,8,48]{2,1,0:T(8,128)} %ids_hbm.1, s32[8,16]{1,0:T(8,128)} %bitcast.8, bf16[2048,256]{1,0:T(8,128)(2,1)} %table_hbm.1, s32[1,256]{1,0:T(1,128)} %bitcast.13, bf16[256,256]{1,0:T(8,128)(2,1)} %item_hbm.1, ...), custom_call_target="tpu_custom_call" | custom-call | flops 1500000000 | bytes 4000000 | tf_op jit(solution)/shard_map/pallas_call | solution.py:482
  24.1 1.7 %shard_map.157 = (bf16[16,256]{1,0:T(8,128)(2,1)}, f32[1,256]{1,0:T(1,128)}, f32[16,256]{1,0:T(8,128)}, f32[256,256]{1,0:T(8,128)}) custom-call(bf16[16,256]{1,0:T(8,128)(2,1)} %get-tuple-element.12.refs_0_, f32[1,256]{1,0:T(1,128)} %get-tuple-element.13.refs_1_, f32[16,256]{1,0:T(8,128)} %get-tuple-element.14.refs_2_, f32[256,256]{1,0:T(8,128)} %get-tuple-element.15.refs_3_), custom_call_target="tpu_custom_call" | custom-call | tf_op jit(solution)/shard_map/pallas_call | solution.py:521

commit v6 on v5

--- a/solution.py
+++ b/solution.py
@@ -239,41 +239,44 @@
             )
             for k in (0, cut)
         ]
-        rows = pl.ds(pl.multiple_of(source * users, users), users)
+        rows = pl.ds(pl.multiple_of(i * users, users), users)
         for h in range(n_hi):
             own = slice(h * few, (h + 1) * few)
             both = jnp.concatenate([top[own], bottom[own]], axis=0)
             counts[rows, h * LANES : (h + 1) * LANES] = both.astype(BF16)
 
-    each(tables, count_source)
-
-    arrived("table")
-    per_step = min(tables, 8)
-    table_all = table_v[...]
-
-    def pool_step(k):
-        rows = per_step * users
-        part = dot_nn(counts[pl.ds(k * rows, rows), :], table_all).astype(BF16)
-        part_send[pl.ds(k * per_step, per_step)] = part.reshape(per_step, users, width)
-
-    each(tables // per_step, pool_step)
-
-    def part_copy(dst_table, owner, src_table):
+    def part_copy(dst_table, owner, slot):
         return pltpu.make_async_remote_copy(
-            src_ref=part_send.at[src_table],
+            src_ref=part_send.at[slot],
             dst_ref=part_recv.at[owner],
-            send_sem=part_ssem.at[src_table],
+            send_sem=part_ssem.at[slot],
             recv_sem=part_rsem.at[owner],
             device_id=(dst_table, s),
             device_id_type=MESH,
         )
 
-    def send_part(i):
-        peer = table_peer(i + 1)
-        part_copy(peer, t, peer).start()
-
-    each(tables - 1, send_part)
-    part_recv[t] = part_send[t]
+    arrived("table")
+    per_step = min(tables, 4)
+
+    def pool_step(k):
+        for j in range(per_step):
+            count_source(k * per_step + j)
+        rows = per_step * users
+        part = dot_nn(counts[pl.ds(k * rows, rows), :], table_v[...]).astype(BF16)
+        part_send[pl.ds(k * per_step, per_step)] = part.reshape(per_step, users, width)
+        for j in range(per_step):
+            i = k * per_step + j
+            if isinstance(i, int):
+                if i > 0:
+                    part_copy(lax.rem(t + tables - i, tables), t, i).start()
+            else:
+
+                @pl.when(i > 0)
+                def _():
+                    part_copy(lax.rem(t + tables - i, tables), t, i).start()
+
+    each(tables // per_step, pool_step)
+    part_recv[t] = part_send[0]
 
     arrived("item", "wh", "wc", "bh", "bc")
     items = item_v[...]
@@ -283,7 +286,7 @@
 
     def take_part(i):
         source = lax.rem(t + tables - 1 - i, tables)
-        part_copy(t, source, t).wait_recv()
+        part_copy(t, source, 0).wait_recv()
 
     each(tables - 1, take_part)
     pooled = jnp.sum(part_recv[...].astype(F32), axis=0) * scale
@@ -402,7 +405,7 @@
     def sent_table(i):
         peer = table_peer(i + 1)
         ids_copy(peer, t, peer).wait_send()
-        part_copy(peer, t, peer).wait_send()
+        part_copy(peer, t, i + 1).wait_send()
 
     def sent_sample(i):
         peer = sample_peer(i + 1)

time: 25.9 us -> 26.3 us (1.015)
  Pallas kernels: 25.1 us -> 25.5 us
    pallas_call x1, Pallas kernels: 23.4 us -> 23.8 us  [body(): pl.pallas_call(functools.partial(kernel, float(history) ** (-0.5)), out_s...]
where the time goes in v6:
time: 26.3 us; the launch traced here: 26.1 us
  Pallas kernels  25.5 us (97%)
  between operations  0.64 us (2%)
    pallas_call x1, Pallas kernels, body(): pl.pallas_call(functools.partial(kernel, float(history) ** (-0.5)), out_s...  23.8 us
    pallas_call x1, Pallas kernels, body(): pl.pallas_call(write_out, out_shape=shapes, in_specs=[hbm] * len(shapes),...  1.72 us

profile of v6, /device:TPU:0, one launch (start us, length us, event | category | flops | bytes accessed | tf_op | source)
XLA Modules:
  0.0 26.1 jit_solution(15841161031007599389)
XLA Ops:
  0.6 23.8 %shard_map.156 = (bf16[16,256]{1,0:T(8,128)(2,1)}, f32[1,256]{1,0:T(1,128)}, f32[16,256]{1,0:T(8,128)}, f32[256,256]{1,0:T(8,128)}) custom-call(s32[16,8,48]{2,1,0:T(8,128)} %ids_hbm.1, s32[8,16]{1,0:T(8,128)} %bitcast.8, bf16[2048,256]{1,0:T(8,128)(2,1)} %table_hbm.1, s32[1,256]{1,0:T(1,128)} %bitcast.13, bf16[256,256]{1,0:T(8,128)(2,1)} %item_hbm.1, ...), custom_call_target="tpu_custom_call" | custom-call | flops 1500000000 | bytes 4000000 | tf_op jit(solution)/shard_map/pallas_call | solution.py:485
  24.4 1.7 %shard_map.157 = (bf16[16,256]{1,0:T(8,128)(2,1)}, f32[1,256]{1,0:T(1,128)}, f32[16,256]{1,0:T(8,128)}, f32[256,256]{1,0:T(8,128)}) custom-call(bf16[16,256]{1,0:T(8,128)(2,1)} %get-tuple-element.12.refs_0_, f32[1,256]{1,0:T(1,128)} %get-tuple-element.13.refs_1_, f32[16,256]{1,0:T(8,128)} %get-tuple-element.14.refs_2_, f32[256,256]{1,0:T(8,128)} %get-tuple-element.15.refs_3_), custom_call_target="tpu_custom_call" | custom-call | tf_op jit(solution)/shard_map/pallas_call | solution.py:524
